TPU v7x, 128 devices: a whole 4x4x4 slice. The times are simulated.
128 devices in a mesh: section: 8 (over z, y_lo), seq: 16 (over y_hi, x, core).
Axes of the slice: x: 4, y: 4 (y_hi: 2, y_lo: 2; y = y_hi * 2 + y_lo), z: 4, core: 2. Of those that a mesh axis runs over, the one named last changes fastest.
Arguments:
- qkv: bfloat16 [8, 1536, 3, 4096], P('section', 'seq'), may hold values from -5 to 5
- cache: bfloat16 [2, 24, 512, 4096], P(None, 'section', None, 'seq'), may hold values from -5 to 5
- window: int32 [8], P('section'), may hold values from 1 to 24, as said below
Outputs:
- attended: bfloat16 [8, 1536, 4096], P('section', 'seq')
- new_cache: bfloat16 [2, 24, 512, 4096], P(None, 'section', None, 'seq')
Inputs may be any that keep to these rules, and one draw needn't show every extreme that they name: `window`: some section attends all 24 cache frames and some section only the newest.
All inputs are finite; a program needn't handle non-finite values.
Results may differ from a plain program's by a relative error of at most 0.02.
Values may be sent and summed in bfloat16 or wider, within the bound.
No kernel may reach another device: no remote copies, remote signals or barrier semaphores. Data moves between devices by JAX's collectives and lax.ppermute only.
A program may use at most 192 MiB of HBM per device.

v0:
```python
import jax
import jax.numpy as jnp
from jax import lax
from jax.sharding import PartitionSpec as P

HD = 128
CF = 3


def passed_along(value, axis, steps):
    count = lax.axis_size(axis)
    leading, last = (max(0, -steps), min(count, count - steps))
    return lax.ppermute(value, axis, [(source, source + steps) for source in range(leading, last)])


def frame_update(state, query, key_block, value_block, valid):
    running, total, accum = state
    scores = jnp.einsum("qhd,khd->qhk", query, key_block, preferred_element_type=jnp.float32)
    scores = scores * query.shape[-1] ** (-0.5)
    masked = jnp.where(valid, scores, -1e30)
    newest = jnp.maximum(running, jnp.max(masked, axis=-1))
    weights = jnp.where(valid, jnp.exp(scores - newest[..., None]), 0.0)
    factor = jnp.exp(running - newest)
    total = total * factor + jnp.sum(weights, axis=-1)
    mixed = jnp.einsum(
        "qhk,khd->qhd",
        weights.astype(jnp.bfloat16),
        value_block,
        preferred_element_type=jnp.float32,
    )
    accum = accum * factor[..., None] + mixed
    return (newest, total, accum)


def per_device(qkv, cache, window):
    denoise_count = lax.axis_size("section")
    tok_rows = qkv.shape[1]
    all_heads = qkv.shape[3] // HD
    local = qkv.reshape(tok_rows, 3, all_heads, HD)
    spread = lax.all_to_all(local, "seq", split_axis=2, concat_axis=0, tiled=True)
    query = spread[:, 0]
    keys = spread[:, 1]
    values = spread[:, 2]
    span_rows = query.shape[0]
    frame = span_rows // CF
    group = query.shape[1]
    query_frame = jnp.arange(span_rows) // frame
    start_state = (
        jnp.full((span_rows, group), -1e30, jnp.float32),
        jnp.zeros((span_rows, group), jnp.float32),
        jnp.zeros((span_rows, group, HD), jnp.float32),
    )
    state = start_state
    for key_frame in range(CF):
        valid = (query_frame >= key_frame)[:, None, None]
        state = frame_update(
            state,
            query,
            keys[key_frame * frame : (key_frame + 1) * frame],
            values[key_frame * frame : (key_frame + 1) * frame],
            valid,
        )
    frames_dev = cache.shape[1]
    cache_frames = frames_dev * denoise_count
    denoise_index = lax.axis_index("section")
    oldest = cache_frames - window[0]
    carry = state
    key_piece = lax.all_gather(cache[0], "section", axis=0, tiled=True)
    value_piece = lax.all_gather(cache[1], "section", axis=0, tiled=True)
    count = key_piece.shape[0]
    key_rows = key_piece.reshape(count, key_piece.shape[1], group, HD)
    value_rows = value_piece.reshape(count, value_piece.shape[1], group, HD)

    def advance(inner, item):
        offset, key_block, value_block = item
        return (frame_update(inner, query, key_block, value_block, offset >= oldest), None)

    carry, _ = lax.scan(advance, carry, (jnp.arange(count, dtype=jnp.int32), key_rows, value_rows))
    state = carry
    running, total, accum = state
    result = (accum / total[..., None]).astype(jnp.bfloat16)
    returned = lax.all_to_all(result, "seq", split_axis=0, concat_axis=1, tiled=True)
    attended = returned.reshape(1, tok_rows, all_heads * HD)
    fresh = jnp.stack([keys, values]).reshape(2, CF, frame, group * HD)
    rolled = passed_along(cache, "section", -1)
    new_cache = jnp.where(denoise_index == denoise_count - 1, fresh, rolled)
    return (attended, new_cache)


def solution(mesh):
    in_specs = (P("section", "seq", None, None), P(None, "section", None, "seq"), P("section"))
    out_specs = (P("section", "seq", None), P(None, "section", None, "seq"))
    return jax.shard_map(
        per_device, mesh=mesh, in_specs=in_specs, out_specs=out_specs, check_vma=False
    )
```

profile of v0, /device:TPU:1, one launch (start us, length us, event | category | flops | bytes accessed | tf_op | source)
XLA Modules:
  0.0 558.6 jit_solution(18189803596885018236)
XLA Ops:
  7.2 2.8 slice_bitcast_fusion.1
  13.7 8.4 %all-to-all-start = ((bf16[96,3,32,128]{3,0,1,2:T(8,128)(2,1)}), bf16[96,3,32,128]{3,0,1,2:T(8,128)(2,1)S(1)}, u32[]{:S(2)}, u32[]{:S(2)}) async-start(bf16[96,3,32,128]{3,0,1,2:T(8,128)(2,1)} %copy.58), calls=%async_computation | async-start | bytes 4718592 | tf_op jit(solution)/shard_map/all_to_all | solution.py:40
  24.1 34.1 %all-to-all-done = bf16[96,3,32,128]{3,0,1,2:T(8,128)(2,1)S(1)} async-done(((bf16[96,3,32,128]{3,0,1,2:T(8,128)(2,1)}), bf16[96,3,32,128]{3,0,1,2:T(8,128)(2,1)S(1)}, u32[]{:S(2)}, u32[]{:S(2)}) %all-to-all-start) | async-done | bytes 2359328 | tf_op jit(solution)/shard_map/all_to_all | solution.py:40
  62.7 2.7 fusion.36
  69.1 3.8 fusion.74
  74.8 2.9 fusion.101
  77.7 124.0 %all-gather.5.cloned.1.call-done = bf16[1,24,512,256]{3,2,0,1:T(8,128)(2,1)} async-done(((bf16[1,3,512,256]{3,2,0,1:T(8,128)(2,1)}), bf16[1,24,512,256]{3,2,0,1:T(8,128)(2,1)}) %all-gather.5.cloned.1.call-update) | async-done | bytes 6291472 | tf_op jit(solution)/shard_map/all_gather | solution.py:68
  201.7 8.7 %copy.65 = bf16[1,24,512,256]{2,3,1,0:T(8,128)(2,1)} copy(bf16[1,24,512,256]{3,2,0,1:T(8,128)(2,1)} %all-gather.5.cloned.1.call-done) | data formatting | bytes 12582912 | tf_op jit(solution)/shard_map/all_gather | solution.py:68
  210.4 123.7 %all-gather.7.cloned.1.call-done = bf16[1,24,512,256]{3,2,0,1:T(8,128)(2,1)} async-done(((bf16[1,3,512,256]{3,2,0,1:T(8,128)(2,1)}), bf16[1,24,512,256]{3,2,0,1:T(8,128)(2,1)}) %all-gather.7.cloned.1.call-update) | async-done | bytes 6291472 | tf_op jit(solution)/shard_map/all_gather | solution.py:69
  334.1 8.7 %copy.81 = bf16[1,24,512,256]{2,3,1,0:T(8,128)(2,1)} copy(bf16[1,24,512,256]{3,2,0,1:T(8,128)(2,1)} %all-gather.7.cloned.1.call-done) | data formatting | bytes 12582912 | tf_op jit(solution)/shard_map/while | solution.py:78
  342.7 173.8 %while.14 = (s32[]{:T(128)}, f32[1536,2]{0,1:T(2,128)S(1)}, f32[1536,2]{0,1:T(2,128)S(1)}, f32[1536,2,128]{0,2,1:T(8,128)S(1)}, s32[24]{0:T(128)S(1)}, /*index=5...) while((s32[]{:T(128)}, f32[1536,2]{0,1:T(2,128)S(1)}, ...), condition=%wide.region_9.10_spmd, body=%wide.region_6.9_spmd.sunk | while | flops 823400448 | bytes 23528572 | solution.py:78
  347.3 2.6 fusion.114
  361.8 2.6 fusion.114
  369.0 2.6 fusion.114
  376.3 2.6 fusion.114
  390.8 2.6 fusion.114
  398.0 2.6 fusion.114
  405.3 2.6 fusion.114
  419.7 2.6 fusion.114
  427.0 2.6 fusion.114
  434.2 2.6 fusion.114
  448.7 2.6 fusion.114
  455.9 2.6 fusion.114
  470.4 2.6 fusion.114
  477.7 2.6 fusion.114
  484.9 2.6 fusion.114
  499.4 2.6 fusion.114
  517.5 7.5 %copy.71 = bf16[1536,2,128]{2,1,0:T(2,128)(2,1)} copy(bf16[1536,2,128]{2,0,1:T(8,128)(2,1)S(1)} %divide_convert_fusion) | data formatting | bytes 1572864 | tf_op jit(solution)/shard_map/convert_element_type | solution.py:81
  525.0 7.3 %all-to-all-start.1 = ((bf16[1536,2,128]{2,1,0:T(2,128)(2,1)}), bf16[1536,2,128]{2,1,0:T(2,128)(2,1)S(1)}, u32[]{:S(2)}, u32[]{:S(2)}) async-start(bf16[1536,2,128]{2,1,0:T(2,128)(2,1)} %copy.71), calls=%async_computation.1 | async-start | bytes 1572864 | tf_op jit(solution)/shard_map/all_to_all | solution.py:82
  532.3 6.7 %copy.74 = bf16[1536,1,2,128]{3,2,0,1:T(2,128)(2,1)S(1)} copy(bf16[1536,1,2,128]{3,0,2,1:T(8,128)(2,1)} %get-tuple-element.124) | data formatting | bytes 1572864 | tf_op jit(solution)/shard_map/slice | solution.py:42
  539.5 6.5 %copy.75 = bf16[1536,1,2,128]{3,2,0,1:T(2,128)(2,1)S(1)} copy(bf16[1536,1,2,128]{3,0,2,1:T(8,128)(2,1)S(1)} %copy-done.1) | data formatting | bytes 1572864 | tf_op jit(solution)/shard_map/slice | solution.py:43
  546.6 2.8 maximum_select_fusion
  (188 shorter events, 134.6 us)
Async XLA Ops:
  7.2 3.6 copy-start.2
  7.2 194.5 %all-gather.5.cloned.1.call-start = ((), (), s32[]{:S(2)}) async-start(), calls=%async_computation.2 | async-start | bytes 7077888 | tf_op jit(solution)/shard_map/all_gather | solution.py:68
  10.0 324.0 %all-gather.7.cloned.1.call-start = ((), (), s32[]{:S(2)}) async-start(), calls=%async_computation.3 | async-start | bytes 7077888 | tf_op jit(solution)/shard_map/all_gather | solution.py:69
  13.7 44.5 %all-to-all-start = ((bf16[96,3,32,128]{3,0,1,2:T(8,128)(2,1)}), bf16[96,3,32,128]{3,0,1,2:T(8,128)(2,1)S(1)}, u32[]{:S(2)}, u32[]{:S(2)}) async-start(bf16[96,3,32,128]{3,0,1,2:T(8,128)(2,1)} %copy.58), calls=%async_computation | async-start | bytes 4718592 | tf_op jit(solution)/shard_map/all_to_all | solution.py:40
  22.1 524.5 %collective-permute-start = (bf16[2,3,512,256]{3,2,1,0:T(8,128)(2,1)}, bf16[2,3,512,256]{3,2,1,0:T(8,128)(2,1)}, u32[]{:S(2)}, u32[]{:S(2)}) collective-permute-start(bf16[2,3,512,256]{3,2,1,0:T(8,128)(2,1)} %param.6), channel_id=1, source_target_pairs={{16,0},{32,16},{48,32},{64,48},{80,64},{96,80},{112,96},{17,1},{33... | collective-permute-start | bytes 4718600 | tf_op jit(solution)/shard_map/ppermute | solution.py:13
  58.3 10.8 %copy-start = (bf16[16,96,3,2,128]{4,1,0,3,2:T(8,128)(2,1)}, bf16[16,96,3,2,128]{4,1,0,3,2:T(8,128)(2,1)S(1)}, u32[]{:S(2)}) copy-start(bf16[16,96,3,2,128]{4,1,0,3,2:T(8,128)(2,1)S(1)} %copy.60) | copy-start | bytes 7077892
  517.0 22.5 %copy-start.1 = (bf16[1536,1,2,128]{3,0,2,1:T(8,128)(2,1)S(1)}, bf16[1536,1,2,128]{3,0,2,1:T(8,128)(2,1)}, u32[]{:S(2)}) copy-start(bf16[1536,1,2,128]{3,0,2,1:T(8,128)(2,1)} %get-tuple-element.125) | copy-start | bytes 2359300
  525.0 24.4 %all-to-all-start.1 = ((bf16[1536,2,128]{2,1,0:T(2,128)(2,1)}), bf16[1536,2,128]{2,1,0:T(2,128)(2,1)S(1)}, u32[]{:S(2)}, u32[]{:S(2)}) async-start(bf16[1536,2,128]{2,1,0:T(2,128)(2,1)} %copy.71), calls=%async_computation.1 | async-start | bytes 1572864 | tf_op jit(solution)/shard_map/all_to_all | solution.py:82
Sparse Core Ops, SparseCore 0:
  10.2 191.4 all-gather.4
  203.9 130.1 all-gather.6
where the time goes:
time: 561 us; the launch traced here: 559 us
  waiting for transfers between devices  282 us (50%)
  matrix products  122 us (22%)
  local copies, waits for them, and re-layouts  66.7 us (12%)
  other arithmetic  38.3 us (7%)
  starting transfers between devices  17.1 us (3%)
  loops' own time  16.8 us (3%)
  between operations  14.9 us (3%)
    all_gather x1, waiting for transfers between devices, per_device(): key_piece = lax.all_gather(cache[0], 'section', axis=0, tiled=True)  124 us
    all_gather x1, waiting for transfers between devices, per_device(): value_piece = lax.all_gather(cache[1], 'section', axis=0, tiled=True)  124 us
    dot_general x27, matrix products, frame_update(): jnp.einsum('qhk,khd->qhd', weights.astype(jnp.bfloat16), value_block, pre...  70 us
    dot_general x27, matrix products, frame_update(): jnp.einsum('qhd,khd->qhk', query, key_block, preferred_element_type=jnp.f...  52.3 us
    all_to_all x1, waiting for transfers between devices, per_device(): lax.all_to_all(local, 'seq', split_axis=2, concat_axis=0, tiled=True)  34.1 us
    reduce_sum x26, other arithmetic, frame_update(): total = total * factor + jnp.sum(weights, axis=-1)  34 us
    another operation x1, loops' own time, per_device(): lax.scan(advance, carry, (jnp.arange(count, dtype=jnp.int32), key_rows, v...  16.8 us
    dynamic_slice x24, local copies, waits for them, and re-layouts, per_device(): lax.scan(advance, carry, (jnp.arange(count, dtype=jnp.int32), key_rows, v...  14.1 us
  transfers between devices with their start and end apart: 5, of which 3 were waited for; matrix products, arithmetic and copies ran while one was open for 40% of the time, Pallas kernels for 0%

commit v1 on v0

--- a/solution.py
+++ b/solution.py
@@ -5,6 +5,13 @@
 
 HD = 128
 CF = 3
+
+
+def exchange_gather(x, axis, dim):
+    size = lax.axis_size(axis)
+    pieces = jnp.stack([x for _ in range(size)])
+    pieces = lax.all_to_all(pieces, axis, split_axis=0, concat_axis=0)
+    return jnp.concatenate(pieces, axis=dim)
 
 
 def passed_along(value, axis, steps):
@@ -65,7 +72,7 @@
     denoise_index = lax.axis_index("section")
     oldest = cache_frames - window[0]
     carry = state
-    key_piece = lax.all_gather(cache[0], "section", axis=0, tiled=True)
+    key_piece = exchange_gather(cache[0], "section", 0)
     value_piece = lax.all_gather(cache[1], "section", axis=0, tiled=True)
     count = key_piece.shape[0]
     key_rows = key_piece.reshape(count, key_piece.shape[1], group, HD)

time: 561 us -> 496 us (0.88)
  waiting for transfers between devices: 282 us -> 215 us
  starting transfers between devices: 17.1 us -> 22.9 us
    all_gather x1 -> x0, waiting for transfers between devices: 124 us -> none  [per_device(): key_piece = lax.all_gather(cache[0], 'section', axis=0, tiled=True)]
    all_gather x1, waiting for transfers between devices: 124 us -> 182 us  [per_device(): value_piece = lax.all_gather(cache[1], 'section', axis=0, tiled=True)]
    all_gather x1 -> x0, local copies, waits for them, and re-layouts: 8.7 us -> none  [per_device(): key_piece = lax.all_gather(cache[0], 'section', axis=0, tiled=True)]
    all_to_all x0 -> x1, starting transfers between devices: none -> 5.8 us  [exchange_gather(): pieces = lax.all_to_all(pieces, axis, split_axis=0, concat_axis=0)]
  transfers between devices with their start and end apart: 5 -> 5, of which waited for: 3 -> 2; matrix products, arithmetic and copies ran while one was open for 40% -> 44% of each run, Pallas kernels for 0% -> 0%
where the time goes in v1:
time: 496 us; the launch traced here: 493 us
  waiting for transfers between devices  215 us (43%)
  matrix products  122 us (25%)
  local copies, waits for them, and re-layouts  64 us (13%)
  other arithmetic  38.1 us (8%)
  starting transfers between devices  22.9 us (5%)
  loops' own time  16.8 us (3%)
  between operations  14.9 us (3%)
    all_gather x1, waiting for transfers between devices, per_device(): value_piece = lax.all_gather(cache[1], 'section', axis=0, tiled=True)  182 us
    dot_general x27, matrix products, frame_update(): jnp.einsum('qhk,khd->qhd', weights.astype(jnp.bfloat16), value_block, pre...  70 us
    dot_general x27, matrix products, frame_update(): jnp.einsum('qhd,khd->qhk', query, key_block, preferred_element_type=jnp.f...  52.3 us
    reduce_sum x26, other arithmetic, frame_update(): total = total * factor + jnp.sum(weights, axis=-1)  33.9 us
    all_to_all x1, waiting for transfers between devices, per_device(): lax.all_to_all(local, 'seq', split_axis=2, concat_axis=0, tiled=True)  32.5 us
    another operation x1, loops' own time, per_device(): lax.scan(advance, carry, (jnp.arange(count, dtype=jnp.int32), key_rows, v...  16.8 us
    dynamic_slice x24, local copies, waits for them, and re-layouts, per_device(): lax.scan(advance, carry, (jnp.arange(count, dtype=jnp.int32), key_rows, v...  14.1 us
    while x3, local copies, waits for them, and re-layouts, per_device(): lax.scan(advance, carry, (jnp.arange(count, dtype=jnp.int32), key_rows, v...  11 us
  transfers between devices with their start and end apart: 5, of which 2 were waited for; matrix products, arithmetic and copies ran while one was open for 44% of the time, Pallas kernels for 0%

profile of v1, /device:TPU:1, one launch (start us, length us, event | category | flops | bytes accessed | tf_op | source)
XLA Modules:
  0.0 493.5 jit_solution(3329094356180938754)
XLA Ops:
  7.2 2.6 slice_bitcast_fusion.1
  14.4 8.4 %all-to-all-start = ((bf16[96,3,32,128]{3,0,1,2:T(8,128)(2,1)}), bf16[96,3,32,128]{3,0,1,2:T(8,128)(2,1)S(1)}, u32[]{:S(2)}, u32[]{:S(2)}) async-start(bf16[96,3,32,128]{3,0,1,2:T(8,128)(2,1)} %copy.57), calls=%async_computation | async-start | bytes 4718592 | tf_op jit(solution)/shard_map/all_to_all | solution.py:47
  26.2 32.5 %all-to-all-done = bf16[96,3,32,128]{3,0,1,2:T(8,128)(2,1)S(1)} async-done(((bf16[96,3,32,128]{3,0,1,2:T(8,128)(2,1)}), bf16[96,3,32,128]{3,0,1,2:T(8,128)(2,1)S(1)}, u32[]{:S(2)}, u32[]{:S(2)}) %all-to-all-start) | async-done | bytes 2359328 | tf_op jit(solution)/shard_map/all_to_all | solution.py:47
  58.7 3.3 stack.10
  62.0 5.8 %all-to-all-start.1 = ((bf16[8,3,512,256]{2,3,1,0:T(8,128)(2,1)}), bf16[8,3,512,256]{2,3,1,0:T(8,128)(2,1)}, u32[]{:S(2)}, u32[]{:S(2)}) async-start(bf16[8,3,512,256]{2,3,1,0:T(8,128)(2,1)} %stack.10), calls=%async_computation.1 | async-start | bytes 12582912 | tf_op jit(solution)/shard_map/all_to_all | solution.py:13
  78.6 3.8 fusion.74
  84.2 2.9 fusion.101
  87.1 182.1 %all-gather.3.cloned.1.call-done = bf16[1,24,512,256]{3,2,0,1:T(8,128)(2,1)} async-done(((bf16[1,3,512,256]{3,2,0,1:T(8,128)(2,1)}), bf16[1,24,512,256]{3,2,0,1:T(8,128)(2,1)}) %all-gather.3.cloned.1.call-update) | async-done | bytes 6291472 | tf_op jit(solution)/shard_map/all_gather | solution.py:76
  269.2 8.7 %copy.79 = bf16[1,24,512,256]{2,3,1,0:T(8,128)(2,1)} copy(bf16[1,24,512,256]{3,2,0,1:T(8,128)(2,1)} %all-gather.3.cloned.1.call-done) | data formatting | bytes 12582912 | tf_op jit(solution)/shard_map/while | solution.py:85
  277.9 173.8 %while.14 = (s32[]{:T(128)}, f32[1536,2]{0,1:T(2,128)S(1)}, f32[1536,2]{0,1:T(2,128)S(1)}, f32[1536,2,128]{0,2,1:T(8,128)S(1)}, s32[24]{0:T(128)S(1)}, /*index=5...) while((s32[]{:T(128)}, f32[1536,2]{0,1:T(2,128)S(1)}, ...), condition=%wide.region_9.10_spmd, body=%wide.region_6.9_spmd.sunk | while | flops 823400448 | bytes 23528572 | solution.py:85
  282.5 2.6 fusion.114
  289.7 2.6 fusion.114
  296.9 2.6 fusion.114
  311.4 2.6 fusion.114
  318.7 2.6 fusion.114
  333.2 2.6 fusion.114
  340.4 2.6 fusion.114
  347.6 2.6 fusion.114
  362.1 2.6 fusion.114
  369.4 2.6 fusion.114
  376.6 2.6 fusion.114
  391.1 2.6 fusion.114
  398.3 2.6 fusion.114
  405.6 2.6 fusion.114
  420.1 2.6 fusion.114
  427.3 2.6 fusion.114
  434.5 2.6 fusion.114
  452.6 7.3 %copy.69 = bf16[1536,2,128]{2,1,0:T(2,128)(2,1)} copy(bf16[1536,2,128]{2,0,1:T(8,128)(2,1)S(1)} %divide_convert_fusion) | data formatting | bytes 1572864 | tf_op jit(solution)/shard_map/convert_element_type | solution.py:88
  459.9 7.3 %all-to-all-start.2 = ((bf16[1536,2,128]{2,1,0:T(2,128)(2,1)}), bf16[1536,2,128]{2,1,0:T(2,128)(2,1)S(1)}, u32[]{:S(2)}, u32[]{:S(2)}) async-start(bf16[1536,2,128]{2,1,0:T(2,128)(2,1)} %copy.69), calls=%async_computation.2 | async-start | bytes 1572864 | tf_op jit(solution)/shard_map/all_to_all | solution.py:89
  467.2 6.7 %copy.72 = bf16[1536,1,2,128]{3,2,0,1:T(2,128)(2,1)S(1)} copy(bf16[1536,1,2,128]{3,0,2,1:T(8,128)(2,1)} %get-tuple-element.124) | data formatting | bytes 1572864 | tf_op jit(solution)/shard_map/slice | solution.py:49
  474.4 6.5 %copy.73 = bf16[1536,1,2,128]{3,2,0,1:T(2,128)(2,1)S(1)} copy(bf16[1536,1,2,128]{3,0,2,1:T(8,128)(2,1)S(1)} %copy-done.1) | data formatting | bytes 1572864 | tf_op jit(solution)/shard_map/slice | solution.py:50
  481.5 2.8 maximum_select_fusion
  (186 shorter events, 136.9 us)
Async XLA Ops:
  7.2 262.0 %all-gather.3.cloned.1.call-start = ((), (), s32[]{:S(2)}) async-start(), calls=%async_computation.3 | async-start | bytes 7077888 | tf_op jit(solution)/shard_map/all_gather | solution.py:76
  14.4 44.3 %all-to-all-start = ((bf16[96,3,32,128]{3,0,1,2:T(8,128)(2,1)}), bf16[96,3,32,128]{3,0,1,2:T(8,128)(2,1)S(1)}, u32[]{:S(2)}, u32[]{:S(2)}) async-start(bf16[96,3,32,128]{3,0,1,2:T(8,128)(2,1)} %copy.57), calls=%async_computation | async-start | bytes 4718592 | tf_op jit(solution)/shard_map/all_to_all | solution.py:47
  22.8 458.7 %collective-permute-start = (bf16[2,3,512,256]{3,2,1,0:T(8,128)(2,1)}, bf16[2,3,512,256]{3,2,1,0:T(8,128)(2,1)}, u32[]{:S(2)}, u32[]{:S(2)}) collective-permute-start(bf16[2,3,512,256]{3,2,1,0:T(8,128)(2,1)} %param.6), channel_id=1, source_target_pairs={{16,0},{32,16},{48,32},{64,48},{80,64},{96,80},{112,96},{17,1},{33... | collective-permute-start | bytes 4718600 | tf_op jit(solution)/shard_map/ppermute | solution.py:20
  62.0 215.9 %all-to-all-start.1 = ((bf16[8,3,512,256]{2,3,1,0:T(8,128)(2,1)}), bf16[8,3,512,256]{2,3,1,0:T(8,128)(2,1)}, u32[]{:S(2)}, u32[]{:S(2)}) async-start(bf16[8,3,512,256]{2,3,1,0:T(8,128)(2,1)} %stack.10), calls=%async_computation.1 | async-start | bytes 12582912 | tf_op jit(solution)/shard_map/all_to_all | solution.py:13
  68.0 10.6 %copy-start = (bf16[16,96,3,2,128]{4,1,0,3,2:T(8,128)(2,1)}, bf16[16,96,3,2,128]{4,1,0,3,2:T(8,128)(2,1)S(1)}, u32[]{:S(2)}) copy-start(bf16[16,96,3,2,128]{4,1,0,3,2:T(8,128)(2,1)S(1)} %copy.59) | copy-start | bytes 7077892
  452.1 22.3 %copy-start.1 = (bf16[1536,1,2,128]{3,0,2,1:T(8,128)(2,1)S(1)}, bf16[1536,1,2,128]{3,0,2,1:T(8,128)(2,1)}, u32[]{:S(2)}) copy-start(bf16[1536,1,2,128]{3,0,2,1:T(8,128)(2,1)} %get-tuple-element.125) | copy-start | bytes 2359300
  459.9 24.4 %all-to-all-start.2 = ((bf16[1536,2,128]{2,1,0:T(2,128)(2,1)}), bf16[1536,2,128]{2,1,0:T(2,128)(2,1)S(1)}, u32[]{:S(2)}, u32[]{:S(2)}) async-start(bf16[1536,2,128]{2,1,0:T(2,128)(2,1)} %copy.69), calls=%async_computation.2 | async-start | bytes 1572864 | tf_op jit(solution)/shard_map/all_to_all | solution.py:89
Sparse Core Ops, SparseCore 0:
  10.2 258.9 all-gather.2
